TPU v7x, 32 devices: a whole 2x2x4 slice. The times are simulated.
32 devices in a mesh: role: 2 (over core), dev: 8 (over z, y), head: 2 (over x).
Axes of the slice: x: 2, y: 2, z: 4, core: 2. Of those that a mesh axis runs over, the one named last changes fastest.
Arguments:
- hidden: bfloat16 [256, 4096], P(('role', 'dev', 'head')), may hold values from -6 to 6
- queries: bfloat16 [256, 64, 128], P(('role', 'dev'), 'head'), as said below
- cache_keys: bfloat16 [256, 128, 4, 128], P(('role', 'dev'), None, 'head'), as said below
- cache_values: bfloat16 [256, 128, 4, 128], P(('role', 'dev'), None, 'head'), may hold values from -6 to 6
- new_keys: bfloat16 [256, 4, 128], P(('role', 'dev'), 'head'), may hold values from -6 to 6
- new_values: bfloat16 [256, 4, 128], P(('role', 'dev'), 'head'), may hold values from -6 to 6
- lengths: int32 [256], P(('role', 'dev')), may hold values from 32 to 128, as said below
- out_proj: bfloat16 [8192, 4096], P('head', 'dev'), may hold values from -0.5 to 0.5
- norm_gain: float32 [4096], replicated, may hold values from 0.1 to 1.9
- expert_gate: bfloat16 [16, 4096, 768], P(('role', 'dev'), None, 'head'), may hold values from -0.09375 to 0.09375
- expert_up: bfloat16 [16, 4096, 768], P(('role', 'dev'), None, 'head'), may hold values from -0.09375 to 0.09375
- expert_down: bfloat16 [16, 768, 4096], P(('role', 'dev'), 'head'), may hold values from -0.21875 to 0.21875
- expert_ids: int32 [256, 8], P(('role', 'dev', 'head')), may hold values from 0 to 15, all different within a row; in each aligned block of 8 rows (0 to 7, 8 to 15, ...) at most 8 rows name the same one
- gate_levels: int32 [256, 8], P(('role', 'dev', 'head')), may hold values from 1 to 255
Outputs:
- layer_out: bfloat16 [256, 4096], P(('role', 'dev', 'head'))
Inputs may be any that keep to these rules, and one draw needn't show every extreme that they name: `queries`: query vectors of the new tokens. `cache_keys`: cached keys of the requests. `lengths`: the first request of each block of 16 rows holds 128 positions and the second holds 32. `expert_ids`: each row names 8 different experts; among the 8 rows of one device no expert is named more than 8 times, a bound that some block reaches.
All inputs are finite; a program needn't handle non-finite values.
Results may differ from a plain program's by a relative error of at most 0.0065.
Values may be sent and summed in bfloat16 or wider, within the bound.
A program may use at most 64 MiB of HBM per device.

v0:
```python
import math

import jax
import jax.numpy as jnp
from jax import lax
from jax.sharding import PartitionSpec as P


def attend_block(query_rows, key_rows, value_rows, key_new, value_new, valid_len):
    row_count = query_rows.shape[0]
    kv_heads = key_rows.shape[2]
    group_size = query_rows.shape[1] // kv_heads
    head_dim = query_rows.shape[2]
    scaling = 1.0 / math.sqrt(head_dim)
    query_f = query_rows.astype(jnp.float32).reshape(row_count, kv_heads, group_size, head_dim)
    scores = jnp.einsum("bhgd,bthd->bhgt", query_f, key_rows.astype(jnp.float32)) * scaling
    scores_new = jnp.einsum("bhgd,bhd->bhg", query_f, key_new.astype(jnp.float32)) * scaling
    positions = jnp.arange(key_rows.shape[1], dtype=jnp.int32)
    usable = (positions[None, :] < valid_len[:, None])[:, None, None, :]
    masked = jnp.where(usable, scores, -1e30)
    highest = jnp.maximum(jnp.max(masked, axis=-1), scores_new)
    exp_terms = jnp.exp(masked - highest[..., None])
    exp_new = jnp.exp(scores_new - highest)
    totals = jnp.sum(exp_terms, axis=-1) + exp_new
    weights = (exp_terms / totals[..., None]).astype(jnp.bfloat16)
    weight_new = (exp_new / totals).astype(jnp.bfloat16)
    blended = jnp.einsum("bhgt,bthd->bhgd", weights, value_rows, preferred_element_type=jnp.float32)
    blended = (
        blended
        + weight_new.astype(jnp.float32)[..., None] * value_new.astype(jnp.float32)[:, :, None, :]
    )
    return blended.astype(jnp.bfloat16).reshape(row_count, kv_heads * group_size * head_dim)


def expert_rows(rows_in, gate_w, up_w, down_w):
    gate_part = jnp.dot(rows_in, gate_w, preferred_element_type=jnp.float32)
    up_part = jnp.dot(rows_in, up_w, preferred_element_type=jnp.float32)
    active = (jax.nn.silu(gate_part) * up_part).astype(jnp.bfloat16)
    return jnp.dot(active, down_w, preferred_element_type=jnp.float32)


def slot_ranks(flat_ids, experts):
    one_hot = (flat_ids[:, None] == jnp.arange(experts, dtype=jnp.int32)[None, :]).astype(jnp.int32)
    return jnp.sum(jnp.cumsum(one_hot, axis=0) * one_hot, axis=1) - 1


def on_device(
    hidden,
    queries,
    cache_keys,
    cache_values,
    new_keys,
    new_values,
    lengths,
    out_proj,
    norm_gain,
    expert_gate,
    expert_up,
    expert_down,
    expert_ids,
    gate_levels,
):
    attended = attend_block(queries, cache_keys, cache_values, new_keys, new_values, lengths)
    columns = jnp.dot(
        lax.all_gather(attended, "dev", axis=0, tiled=True),
        out_proj,
        preferred_element_type=jnp.float32,
    )
    dev_count = lax.axis_size("dev")
    head_count = lax.axis_size("head")
    experts = lax.axis_size("role") * dev_count
    col_width = out_proj.shape[1]
    width = dev_count * col_width
    projected = lax.all_to_all(columns, ("dev", "head"), split_axis=0, concat_axis=1, tiled=True)
    tokens = projected.shape[0]
    summed = jnp.sum(projected.reshape(tokens, dev_count, head_count, col_width), axis=2).reshape(
        tokens, width
    )
    residual = hidden.astype(jnp.float32) + summed
    normed = (
        residual
        * lax.rsqrt(jnp.mean(residual * residual, axis=-1, keepdims=True) + 1e-06)
        * norm_gain
    ).astype(jnp.bfloat16)
    top_k = expert_ids.shape[1]
    capacity = max(2, 2 * tokens * top_k // experts)
    own_ids = expert_ids.reshape(-1)
    own_ranks = slot_ranks(own_ids, experts)
    pair_rows, pair_ids = (
        lax.all_gather(normed, "head", axis=0, tiled=True),
        lax.all_gather(expert_ids, "head", axis=0, tiled=True),
    )
    pair_flat = pair_ids.reshape(head_count, tokens * top_k)
    pair_ranks = jax.vmap(lambda id_row: slot_ranks(id_row, experts))(pair_flat)
    pair_ranks = pair_ranks + capacity * jnp.arange(head_count, dtype=jnp.int32)[:, None]
    rows_from = jnp.arange(head_count * tokens * top_k, dtype=jnp.int32) // top_k
    outgoing = (
        jnp.zeros((experts, head_count * capacity, width), jnp.bfloat16)
        .at[pair_flat.reshape(-1), pair_ranks.reshape(-1)]
        .set(pair_rows[rows_from])
    )
    incoming = lax.all_to_all(outgoing, ("role", "dev"), split_axis=0, concat_axis=0, tiled=True)
    sources = incoming.shape[0]
    slot_total = incoming.shape[1]
    partial_value = expert_rows(
        incoming.reshape(sources * slot_total, width), expert_gate[0], expert_up[0], expert_down[0]
    )
    partial_value = partial_value.reshape(sources, slot_total, width).astype(jnp.bfloat16)
    arrived = lax.all_to_all(
        partial_value, ("role", "dev"), split_axis=0, concat_axis=0, tiled=True
    )
    arrived = (
        lax.psum_scatter(arrived, "head", scatter_dimension=1, tiled=True)
        .astype(jnp.float32)
        .astype(jnp.bfloat16)
    )
    picked = arrived[own_ids, own_ranks].astype(jnp.float32).reshape(tokens, top_k, width)
    levels = gate_levels.astype(jnp.float32)
    shares = levels / jnp.sum(levels, axis=1, keepdims=True)
    return (residual + jnp.sum(shares[..., None] * picked, axis=1)).astype(jnp.bfloat16)


def solution(mesh):
    placed = (
        P(("role", "dev", "head"), None),
        P(("role", "dev"), "head", None),
        P(("role", "dev"), None, "head", None),
        P(("role", "dev"), None, "head", None),
        P(("role", "dev"), "head", None),
        P(("role", "dev"), "head", None),
        P(("role", "dev")),
        P("head", "dev"),
        P(),
        P(("role", "dev"), None, "head"),
        P(("role", "dev"), None, "head"),
        P(("role", "dev"), "head", None),
        P(("role", "dev", "head"), None),
        P(("role", "dev", "head"), None),
    )
    return jax.shard_map(
        on_device,
        mesh=mesh,
        in_specs=placed,
        out_specs=P(("role", "dev", "head"), None),
        check_vma=False,
    )
```

profile of v0, /device:TPU:0, one launch (start us, length us, event | category | flops | bytes accessed | tf_op | source)
XLA Modules:
  0.0 275.4 jit_solution(3910990733960012574)
XLA Ops:
  6.5 0.9 iota_compare_fusion.2
  7.4 1.1 fusion.21
  8.6 2.1 fusion.33
  10.7 0.3 fusion.16
  11.0 0.7 convert_element_type.55
  11.7 1.7 fusion.12
  13.4 0.7 copy.40
  14.1 5.2 %all_gather.10 = s32[16,8]{1,0:T(8,128)S(1)} all-gather(s32[8,8]{1,0:T(8,128)S(1)} %copy-done.2), channel_id=1, replica_groups=mesh['role'=2,'dev'=8,'head'=2] {'head'}, dimensions={0}, use_global_device_ids=true | all-gather | bytes 768 | tf_op jit(solution)/shard_map/all_gather | solution.py:91
  19.7 0.2 select_reduce_fusion
  19.9 37.4 %all-gather.2.cloned.1.call-done = bf16[128,4096]{1,0:T(8,128)(2,1)} async-done(((bf16[16,4096]{1,0:T(8,128)(2,1)}), bf16[128,4096]{1,0:T(8,128)(2,1)}) %all-gather.2.cloned.1.call-update) | async-done | bytes 1048592 | tf_op jit(solution)/shard_map/all_gather | solution.py:65
  57.2 4.0 %convolution_bitcast_fusion = f32[16,8,512]{2,1,0:T(8,128)} fusion(bf16[128,4096]{1,0:T(8,128)(2,1)} %all-gather.2.cloned.1.call-done, bf16[4096,512]{1,0:T(8,128)(2,1)} %param.21), kind=kOutput, calls=%fused_computation.11 | convolution fusion | flops 536870912 | bytes 5505024 | tf_op jit(solution)/shard_map/dot_general | solution.py:64
  61.2 4.4 %all-to-all-start = ((f32[16,8,512]{2,1,0:T(8,128)}), f32[16,8,512]{2,1,0:T(8,128)}, u32[]{:S(2)}, u32[]{:S(2)}) async-start(f32[16,8,512]{2,1,0:T(8,128)} %convolution_bitcast_fusion), calls=%async_computation | async-start | bytes 524288 | tf_op jit(solution)/shard_map/all_to_all | solution.py:74
  65.9 8.2 %all-to-all-done = f32[16,8,512]{2,1,0:T(8,128)} async-done(((f32[16,8,512]{2,1,0:T(8,128)}), f32[16,8,512]{2,1,0:T(8,128)}, u32[]{:S(2)}, u32[]{:S(2)}) %all-to-all-start) | async-done | bytes 262176 | tf_op jit(solution)/shard_map/all_to_all | solution.py:74
  74.1 1.0 bitcast_reduce_fusion
  75.4 4.9 %all_gather.11 = bf16[16,4096]{1,0:T(8,128)(2,1)S(1)} all-gather(bf16[8,4096]{1,0:T(8,128)(2,1)S(1)} %multiply_convert_fusion), channel_id=1, replica_groups=mesh['role'=2,'dev'=8,'head'=2] {'head'}, dimensions={0}, use_global_device_ids=true | all-gather | bytes 196608 | tf_op jit(solution)/shard_map/all_gather | solution.py:90
  80.3 2.2 gather_fusion
  82.5 1.6 broadcast_in_dim.16
  84.1 34.4 %scatter_fusion = bf16[16,16,4096]{2,1,0:T(8,128)(2,1)} fusion(bf16[16,16,4096]{2,1,0:T(8,128)(2,1)} %broadcast_in_dim.16, s32[128]{0:T(128)S(1)} %fusion.31, bf16[128,4096]{1,0:T(8,128)(2,1)} %gather_fusion), kind=kCustom, calls=%fused_computation.2 | custom fusion | bytes 3146752 | tf_op jit(solution)/shard_map/scatter | solution.py:100
  118.5 53.5 %all_to_all.26 = bf16[16,16,4096]{2,1,0:T(8,128)(2,1)S(1)} all-to-all(bf16[16,16,4096]{2,1,0:T(8,128)(2,1)} %scatter_fusion), channel_id=1, replica_groups=mesh['role'=2,'dev'=8,'head'=2] {'role','dev'}, dimensions={0} | all-to-all | bytes 4194304 | tf_op jit(solution)/shard_map/all_to_all | solution.py:102
  172.0 1.3 fusion.3
  173.3 0.6 copy-done.6
  173.9 1.3 fusion.8
  175.2 1.3 convolution_convert_fusion
  176.5 52.1 %all_to_all.27 = bf16[16,16,4096]{2,1,0:T(8,128)(2,1)S(1)} all-to-all(bf16[16,16,4096]{2,1,0:T(8,128)(2,1)S(1)} %convolution_convert_fusion), channel_id=1, replica_groups=mesh['role'=2,'dev'=8,'head'=2] {'role','dev'}, dimensions={0} | all-to-all | bytes 4194304 | tf_op jit(solution)/shard_map/all_to_all | solution.py:109
  228.6 1.5 copy.26
  230.6 0.2 select_reduce_fusion.1
  230.8 28.8 %reduce-scatter.4.cloned.1.call-done = bf16[8,65536]{1,0:T(8,128)(2,1)} async-done(((bf16[16,65536]{1,0:T(8,128)(2,1)}), bf16[8,65536]{1,0:T(8,128)(2,1)}) %reduce-scatter.4.cloned.1.call-update) | async-done | bytes 1048592
  259.6 1.8 copy.39
  261.4 1.6 copy.24
  263.0 3.4 %gather_fusion.1 = bf16[64,4096]{1,0:T(8,128)(2,1)} fusion(bf16[16,8,4096]{2,1,0:T(8,128)(2,1)} %copy.24, s32[64]{0:T(128)S(1)} %fusion.30), kind=kCustom, calls=%fused_computation.1 | custom fusion | bytes 1049088 | tf_op jit(solution)/shard_map/gather | solution.py:117
  266.4 1.5 fusion.13
  267.9 0.7 add_convert_fusion
  (39 shorter events, 1.5 us)
Async XLA Ops:
  6.5 168.6 %copy-start = (bf16[1,384,4096]{2,1,0:T(8,128)(2,1)S(1)}, bf16[1,384,4096]{2,1,0:T(8,128)(2,1)}, u32[]{:S(2)}) copy-start(bf16[1,384,4096]{2,1,0:T(8,128)(2,1)} %param.25) | copy-start | bytes 9437188
  6.5 7.6 %copy-start.2 = (s32[8,8]{1,0:T(8,128)S(1)}, s32[8,8]{1,0:T(8,128)}, u32[]{:S(2)}) copy-start(s32[8,8]{1,0:T(8,128)} %param.26) | copy-start | bytes 772
  6.5 50.7 %all-gather.2.cloned.1.call-start = ((), (), s32[]{:S(2)}) async-start(), calls=%async_computation.4 | async-start | bytes 1179648 | tf_op jit(solution)/shard_map/all_gather | solution.py:65
  19.8 55.3 %copy-start.1 = (bf16[8,4096]{1,0:T(8,128)(2,1)S(1)}, bf16[8,4096]{1,0:T(8,128)(2,1)}, u32[]{:S(2)}) copy-start(bf16[8,4096]{1,0:T(8,128)(2,1)} %param.14) | copy-start | bytes 196612
  19.8 55.5 %copy-start.3 = (f32[4096]{0:T(1024)S(1)}, f32[4096]{0:T(1024)}, u32[]{:S(2)}) copy-start(f32[4096]{0:T(1024)} %param.22) | copy-start | bytes 49156
  61.2 13.0 %all-to-all-start = ((f32[16,8,512]{2,1,0:T(8,128)}), f32[16,8,512]{2,1,0:T(8,128)}, u32[]{:S(2)}, u32[]{:S(2)}) async-start(f32[16,8,512]{2,1,0:T(8,128)} %convolution_bitcast_fusion), calls=%async_computation | async-start | bytes 524288 | tf_op jit(solution)/shard_map/all_to_all | solution.py:74
  65.6 194.0 %reduce-scatter.4.cloned.1.call-start = ((), (), s32[]{:S(2)}) async-start(), calls=%async_computation.5 | async-start | bytes 3145728
  118.5 53.6 %copy-start.5 = (bf16[1,4096,384]{2,1,0:T(8,128)(2,1)S(1)}, bf16[1,4096,384]{2,1,0:T(8,128)(2,1)}, u32[]{:S(2)}) copy-start(bf16[1,4096,384]{2,1,0:T(8,128)(2,1)} %param.23) | copy-start | bytes 9437188
  172.0 1.9 copy-start.6
  228.6 1.8 copy-start.4
Sparse Core Ops, SparseCore 0:
  14.2 42.9 all-gather.1
  230.2 29.3 reduce-scatter.3
where the time goes:
time: 276 us; the launch traced here: 275 us
  blocking collectives  116 us (42%)
  waiting for transfers between devices  74.4 us (27%)
  local copies, waits for them, and re-layouts  48.1 us (17%)
  between operations  13.6 us (5%)
  matrix products  12.6 us (5%)
  other arithmetic  6.33 us (2%)
  starting transfers between devices  4.46 us (2%)
    all_to_all x1, blocking collectives, on_device(): lax.all_to_all(outgoing, ('role', 'dev'), split_axis=0, concat_axis=0, ti...  53.5 us
    all_to_all x1, blocking collectives, on_device(): lax.all_to_all(partial_value, ('role', 'dev'), split_axis=0, concat_axis=...  52.1 us
    all_gather x1, waiting for transfers between devices, on_device(): lax.all_gather(attended, 'dev', axis=0, tiled=True)  37.4 us
    scatter x1, local copies, waits for them, and re-layouts, on_device(): outgoing = jnp.zeros((experts, head_count * capacity, width), jnp.bfloat1...  34.4 us
    unnamed x3, waiting for transfers between devices  28.8 us
    all_to_all x1, waiting for transfers between devices, on_device(): lax.all_to_all(columns, ('dev', 'head'), split_axis=0, concat_axis=1, til...  8.23 us
    unnamed x18, local copies, waits for them, and re-layouts  6.23 us
  transfers between devices with their start and end apart: 3, of which 3 were waited for; matrix products, arithmetic and copies ran while one was open for 1% of the time, Pallas kernels for 0%

commit v1 on v0

--- a/solution.py
+++ b/solution.py
@@ -1,9 +1,14 @@
+import functools
 import math
 
 import jax
 import jax.numpy as jnp
 from jax import lax
+from jax.experimental import pallas as pl
+from jax.experimental.pallas import tpu as pltpu
 from jax.sharding import PartitionSpec as P
+
+MESH = pl.DeviceIdType.MESH
 
 
 def attend_block(query_rows, key_rows, value_rows, key_new, value_new, valid_len):
@@ -44,6 +49,430 @@
     return jnp.sum(jnp.cumsum(one_hot, axis=0) * one_hot, axis=1) - 1
 
 
+def place_of(role, first, second, depth):
+    head = first * (1 - role) + second * role
+    low = second * (1 - role) + first * role
+    return (role, 2 * depth + low, head)
+
+
+def partner_depths(depth):
+    return (depth, depth + 1 - 2 * (depth % 2), depth + 2 - 4 * (depth // 2), 3 - depth)
+
+
+def layer_kernel(
+    pieces,
+    att_ref,
+    hidden_ref,
+    gain_ref,
+    ids_ref,
+    levels_ref,
+    proj_hbm,
+    gate_hbm,
+    up_hbm,
+    down_hbm,
+    out_ref,
+    gathered,
+    proj_ref,
+    gate_ref,
+    up_ref,
+    down_ref,
+    col_out,
+    col_in,
+    residual_ref,
+    token_ref,
+    low_ref,
+    high_ref,
+    part_ref,
+    core_in,
+    first_out,
+    first_in,
+    second_out,
+    second_in,
+    depth_out,
+    depth_in,
+    weight_sems,
+    att_send,
+    att_recv,
+    col_send,
+    col_recv,
+    tok_send,
+    tok_recv,
+    sum_send,
+    sum_recv,
+):
+    role, dev, head = lax.axis_index("role"), lax.axis_index("dev"), lax.axis_index("head")
+    group_count = gathered.shape[0]
+    width = residual_ref.shape[1]
+    half = width // 2
+    member = dev * 2 + head
+    members = group_count * 2
+    low, depth = dev % 2, dev // 2
+    first = head * (1 - role) + low * role
+    second = low * (1 - role) + head * role
+    depths = partner_depths(depth)
+    other_core = (1 - role, dev, head)
+
+    loads = [
+        pltpu.make_async_copy(source, target, weight_sems.at[number])
+        for number, (source, target) in enumerate(
+            ((proj_hbm, proj_ref), (gate_hbm, gate_ref), (up_hbm, up_ref), (down_hbm, down_ref))
+        )
+    ]
+    for load in loads:
+        load.start()
+
+    barrier = pltpu.get_barrier_semaphore()
+
+    def greet(step, carry):
+        target = (member + step) % members
+        pl.semaphore_signal(
+            barrier, inc=1, device_id=(role, target // 2, target % 2), device_id_type=MESH
+        )
+        return carry
+
+    lax.fori_loop(1, members, greet, 0)
+    pl.semaphore_signal(barrier, inc=1, device_id=other_core, device_id_type=MESH)
+    gathered[dev] = att_ref[...]
+    pl.semaphore_wait(barrier, members)
+
+    def att_copy(depth_from, target, number):
+        block = gathered.at[2 * depth_from + low]
+        return pltpu.make_async_remote_copy(
+            src_ref=block,
+            dst_ref=block,
+            send_sem=att_send.at[number],
+            recv_sem=att_recv.at[number],
+            device_id=target,
+            device_id_type=MESH,
+        )
+
+    beside = (role, 2 * depth + 1 - low, head)
+    along = [att_copy(depth, (role, 2 * depths[k] + low, head), k - 1) for k in (1, 2, 3)]
+    across = [att_copy(depths[k], beside, 3 + k) for k in range(4)]
+    across[0].start()
+    for copy in along:
+        copy.start()
+    for k in (1, 2, 3):
+        along[k - 1].wait_recv()
+        across[k].start()
+    for copy in across:
+        copy.wait_recv()
+
+    loads[0].wait()
+    rows = gathered[...].reshape(group_count * gathered.shape[1], gathered.shape[2])
+    columns = jnp.dot(rows, proj_ref[...], preferred_element_type=jnp.float32)
+    col_width = columns.shape[1]
+    tokens = residual_ref.shape[0]
+    columns = columns.reshape(members, tokens, col_width)
+    col_out[...] = jnp.concatenate(
+        [columns[:, :, : col_width // 2], columns[:, :, col_width // 2 :]], axis=1
+    ).astype(jnp.bfloat16)
+
+    def col_copy(step):
+        target = (member + step) % members
+        return pltpu.make_async_remote_copy(
+            src_ref=col_out.at[target],
+            dst_ref=col_in.at[member],
+            send_sem=col_send.at[step - 1],
+            recv_sem=col_recv.at[step - 1],
+            device_id=(role, target // 2, target % 2),
+            device_id_type=MESH,
+        )
+
+    def col_start(step, carry):
+        col_copy(step).start()
+        return carry
+
+    def col_arrive(step, carry):
+        col_copy(step).wait_recv()
+        return carry
+
+    lax.fori_loop(1, members, col_start, 0)
+    col_in[member] = col_out[member]
+    lax.fori_loop(1, members, col_arrive, 0)
+
+    for block in range(group_count):
+        both = col_in[2 * block].astype(jnp.float32) + col_in[2 * block + 1].astype(jnp.float32)
+        for side in range(2):
+            edge = block * col_width + side * (col_width // 2)
+            span = slice(edge, edge + col_width // 2)
+            residual_ref[:, span] = (
+                hidden_ref[:, span].astype(jnp.float32) + both[side * tokens : (side + 1) * tokens]
+            )
+    residual = residual_ref[...]
+    square = jnp.sum(residual * residual, axis=-1, keepdims=True) / width
+    normed = residual * lax.rsqrt(square + 1e-06) * gain_ref[...]
+    lanes = lax.broadcasted_iota(jnp.int32, (tokens, 128), 1)
+    named = jnp.zeros((tokens, 128), jnp.float32)
+    for k in range(ids_ref.shape[1]):
+        level = levels_ref[:, k : k + 1].astype(jnp.float32)
+        named = named + jnp.where(lanes == ids_ref[:, k : k + 1], level, 0.0)
+    slot = role * 16 + first * 8 + second * 4 + depth
+    token_ref[slot, :, :half] = jnp.concatenate(
+        [normed[:, :half], normed[:, half:]], axis=0
+    ).astype(jnp.bfloat16)
+    token_ref[slot, :, half:] = jnp.concatenate(
+        [named, jnp.zeros((tokens, 128), jnp.float32)], axis=0
+    ).astype(jnp.bfloat16)
+
+    def token_copy(start, count, target, number):
+        block = token_ref.at[pl.ds(start, count)]
+        return pltpu.make_async_remote_copy(
+            src_ref=block,
+            dst_ref=block,
+            send_sem=tok_send.at[number],
+            recv_sem=tok_recv.at[number],
+            device_id=target,
+            device_id_type=MESH,
+        )
+
+    def slot_of(first_at, second_at, depth_at):
+        return role * 16 + first_at * 8 + second_at * 4 + depth_at
+
+    second_side = place_of(role, first, 1 - second, depth)
+    first_side = place_of(role, 1 - first, second, depth)
+    own = [slot_of(first, second, depths[k]) for k in range(4)]
+    near = [slot_of(first, 1 - second, depths[k]) for k in range(4)]
+    to_depth = [
+        token_copy(own[0], 1, place_of(role, first, second, depths[k]), k - 1) for k in (1, 2, 3)
+    ]
+    to_second = [token_copy(own[k], 1, second_side, 3 + k) for k in range(4)]
+    to_first = [token_copy(own[k], 1, first_side, 7 + k) for k in range(4)]
+    to_first = to_first + [token_copy(near[k], 1, first_side, 11 + k) for k in range(4)]
+    to_core = [
+        token_copy(slot_of(*corner, 0), 4, other_core, 15 + number)
+        for number, corner in enumerate(
+            ((first, second), (first, 1 - second), (1 - first, second), (1 - first, 1 - second))
+        )
+    ]
+    to_second[0].start()
+    to_first[0].start()
+    for copy in to_depth:
+        copy.start()
+    for k in (1, 2, 3):
+        to_depth[k - 1].wait_recv()
+        to_second[k].start()
+        to_first[k].start()
+    to_core[0].start()
+    for k in range(4):
+        to_second[k].wait_recv()
+        to_first[4 + k].start()
+    to_core[1].start()
+    for k in range(4):
+        to_first[k].wait_recv()
+    to_core[2].start()
+    for k in range(4, 8):
+        to_first[k].wait_recv()
+    to_core[3].start()
+    for copy in to_core:
+        copy.wait_recv()
+
+    def unfold(pair, carry):
+        one = token_ref[2 * pair, :, :half].astype(jnp.float32)
+        two = token_ref[2 * pair + 1, :, :half].astype(jnp.float32)
+        low_ref[pair] = jnp.concatenate([one[:tokens], two[:tokens]], axis=0).astype(jnp.bfloat16)
+        high_ref[pair] = jnp.concatenate([one[tokens:], two[tokens:]], axis=0).astype(jnp.bfloat16)
+        return carry
+
+    pairs = low_ref.shape[0]
+    lax.fori_loop(0, pairs, unfold, 0)
+    total_rows = pairs * 2 * tokens
+    table = token_ref[:, :, half:].astype(jnp.float32)[:, :tokens].reshape(total_rows, 128)
+    mine = lax.broadcasted_iota(jnp.int32, (total_rows, 128), 1) == role * group_count + dev
+    share = jnp.sum(jnp.where(mine, table, 0.0), axis=1, keepdims=True) / jnp.sum(
+        table, axis=1, keepdims=True
+    )
+    left = low_ref[...].reshape(total_rows, half)
+    right = high_ref[...].reshape(total_rows, half)
+
+    def through(weight_ref):
+        return jnp.dot(left, weight_ref[:half], preferred_element_type=jnp.float32) + jnp.dot(
+            right, weight_ref[half:], preferred_element_type=jnp.float32
+        )
+
+    loads[1].wait()
+    gate_part = through(gate_ref)
+    loads[2].wait()
+    up_part = through(up_ref)
+    active = (gate_part / (1.0 + jnp.exp(-gate_part)) * up_part).astype(jnp.bfloat16)
+    loads[3].wait()
+
+    span_width = half // pieces
+
+    def sum_copy(source, target, device, number):
+        return pltpu.make_async_remote_copy(
+            src_ref=source,
+            dst_ref=target,
+            send_sem=sum_send.at[number],
+            recv_sem=sum_recv.at[number],
+            device_id=device,
+            device_id_type=MESH,
+        )
+
+    core_sums = [
+        sum_copy(part_ref.at[p, pl.ds((1 - role) * 16, 16)], core_in.at[p], other_core, 6 * p)
+        for p in range(pieces)
+    ]
+    first_sums = [
+        sum_copy(first_out.at[p], first_in.at[p], first_side, 6 * p + 1) for p in range(pieces)
+    ]
+    second_sums = [
+        sum_copy(second_out.at[p], second_in.at[p], second_side, 6 * p + 2) for p in range(pieces)
+    ]
+    depth_sums = [
+        [
+            sum_copy(
+                depth_out.at[p, k - 1],
+                depth_in.at[p, k - 1],
+                place_of(role, first, second, depths[k]),
+                6 * p + 2 + k,
+            )
+            for k in (1, 2, 3)
+        ]
+        for p in range(pieces)
+    ]
+
+    def produce(p):
+        sides = []
+        for side in range(2):
+            edge = side * half + p * span_width
+            product = jnp.dot(
+                active, down_ref[:, edge : edge + span_width], preferred_element_type=jnp.float32
+            )
+            sides.append((product * share).reshape(2 * pairs, tokens, span_width))
+        part_ref[p] = jnp.concatenate(sides, axis=1).astype(jnp.bfloat16)
+        core_sums[p].start()
+
+    def core_total(p, start, count):
+        return part_ref[p, pl.ds(role * 16 + start, count)].astype(jnp.float32) + core_in[
+            p, pl.ds(start, count)
+        ].astype(jnp.float32)
+
+    def pass_first(p):
+        core_sums[p].wait_recv()
+        first_out[p] = core_total(p, (1 - first) * 8, 8).astype(jnp.bfloat16)
+        first_sums[p].start()
+
+    def first_total(p, second_at, depth_at, count):
+        start = second_at * 4 + depth_at
+        return core_total(p, first * 8 + start, count) + first_in[p, pl.ds(start, count)].astype(
+            jnp.float32
+        )
+
+    def pass_second(p):
+        first_sums[p].wait_recv()
+        second_out[p] = first_total(p, 1 - second, 0, 4).astype(jnp.bfloat16)
+        second_sums[p].start()
+
+    def second_total(p, depth_at):
+        return first_total(p, second, depth_at, 1)[0] + second_in[p, depth_at].astype(jnp.float32)
+
+    def pass_depth(p):
+        second_sums[p].wait_recv()
+        for k in (1, 2, 3):
+            depth_out[p, k - 1] = second_total(p, depths[k]).astype(jnp.bfloat16)
+            depth_sums[p][k - 1].start()
+
+    def finish(p):
+        total = second_total(p, depth)
+        for k in range(3):
+            depth_sums[p][k].wait_recv()
+            total = total + depth_in[p, k].astype(jnp.float32)
+        for side in range(2):
+            edge = side * half + p * span_width
+            span = slice(edge, edge + span_width)
+            out_ref[:, span] = (
+                residual_ref[:, span] + total[side * tokens : (side + 1) * tokens]
+            ).astype(jnp.bfloat16)
+
+    steps = (produce, pass_first, pass_second, pass_depth, finish)
+    for turn in range(pieces + len(steps) - 1):
+        for lag, step in enumerate(steps):
+            if 0 <= turn - lag < pieces:
+                step(turn - lag)
+
+    def col_sent(step, carry):
+        col_copy(step).wait_send()
+        return carry
+
+    lax.fori_loop(1, members, col_sent, 0)
+    sent = along + across + to_depth + to_second + to_first + to_core
+    sent = sent + core_sums + first_sums + second_sums
+    for group in depth_sums:
+        sent = sent + group
+    for copy in sent:
+        copy.wait_send()
+
+
+def fused_layer(
+    attended, hidden, norm_gain, expert_ids, gate_levels, out_proj, gate_w, up_w, down_w
+):
+    pieces = 4
+    tokens, width = hidden.shape
+    half = width // 2
+    rows, inner = attended.shape
+    col_width = out_proj.shape[1]
+    dev_count = lax.axis_size("dev")
+    hidden_units = gate_w.shape[1]
+    span = half // pieces
+    bf16 = jnp.bfloat16
+    vmem = pl.BlockSpec(memory_space=pltpu.VMEM)
+    anywhere = pl.BlockSpec(memory_space=pl.ANY)
+    sems = pltpu.SemaphoreType.DMA
+    return pl.pallas_call(
+        functools.partial(layer_kernel, pieces),
+        out_shape=jax.ShapeDtypeStruct((tokens, width), bf16),
+        in_specs=[vmem] * 5 + [anywhere] * 4,
+        out_specs=vmem,
+        scratch_shapes=[
+            pltpu.VMEM((dev_count, rows, inner), bf16),
+            pltpu.VMEM(out_proj.shape, bf16),
+            pltpu.VMEM((width, hidden_units), bf16),
+            pltpu.VMEM((width, hidden_units), bf16),
+            pltpu.VMEM((hidden_units, width), bf16),
+            pltpu.VMEM((2 * dev_count, 2 * tokens, col_width // 2), bf16),
+            pltpu.VMEM((2 * dev_count, 2 * tokens, col_width // 2), bf16),
+            pltpu.VMEM((tokens, width), jnp.float32),
+            pltpu.VMEM((4 * dev_count, 2 * tokens, half + 128), bf16),
+            pltpu.VMEM((2 * dev_count, 2 * tokens, half), bf16),
+            pltpu.VMEM((2 * dev_count, 2 * tokens, half), bf16),
+            pltpu.VMEM((pieces, 32, 2 * tokens, span), bf16),
+            pltpu.VMEM((pieces, 16, 2 * tokens, span), bf16),
+            pltpu.VMEM((pieces, 8, 2 * tokens, span), bf16),
+            pltpu.VMEM((pieces, 8, 2 * tokens, span), bf16),
+            pltpu.VMEM((pieces, 4, 2 * tokens, span), bf16),
+            pltpu.VMEM((pieces, 4, 2 * tokens, span), bf16),
+            pltpu.VMEM((pieces, 3, 2 * tokens, span), bf16),
+            pltpu.VMEM((pieces, 3, 2 * tokens, span), bf16),
+            sems((4,)),
+            sems((7,)),
+            sems((7,)),
+            sems((2 * dev_count - 1,)),
+            sems((2 * dev_count - 1,)),
+            sems((19,)),
+            sems((19,)),
+            sems((6 * pieces,)),
+            sems((6 * pieces,)),
+        ],
+        compiler_params=pltpu.CompilerParams(
+            collective_id=0, has_side_effects=True, vmem_limit_bytes=56 * 1024 * 1024
+        ),
+        cost_estimate=pl.CostEstimate(
+            flops=3 * 2 * 256 * width * hidden_units, bytes_accessed=16 << 20, transcendentals=0
+        ),
+    )(
+        attended,
+        hidden,
+        norm_gain.reshape(1, width),
+        expert_ids,
+        gate_levels,
+        out_proj,
+        gate_w,
+        up_w,
+        down_w,
+    )
+
+
 def on_device(
     hidden,
     queries,
@@ -61,6 +490,19 @@
     gate_levels,
 ):
     attended = attend_block(queries, cache_keys, cache_values, new_keys, new_values, lengths)
+    sizes = tuple(lax.axis_size(name) for name in ("role", "dev", "head"))
+    if sizes == (2, 8, 2) and hidden.shape[0] == 8 and queries.shape[0] == 16:
+        return fused_layer(
+            attended,
+            hidden,
+            norm_gain,
+            expert_ids,
+            gate_levels,
+            out_proj,
+            expert_gate[0],
+            expert_up[0],
+            expert_down[0],
+        )
     columns = jnp.dot(
         lax.all_gather(attended, "dev", axis=0, tiled=True),
         out_proj,

time: 276 us -> 79.7 us (0.29)
  blocking collectives: 116 us -> 0 us
  waiting for transfers between devices: 74.4 us -> 0 us
  Pallas kernels: 0 us -> 70.8 us
  local copies, waits for them, and re-layouts: 48.1 us -> 2.18 us
  between operations: 13.6 us -> 0.04 us
  matrix products: 12.6 us -> 4.39 us
  starting transfers between devices: 4.46 us -> 0 us
  other arithmetic: 6.33 us -> 1.88 us
    all_to_all x2 -> x0, blocking collectives: 106 us -> none  [the longest x1 53.5 us: on_device(): lax.all_to_all(outgoing, ('role', 'dev'), split_axis=0, concat_axis=0, ti...]
    pallas_call x0 -> x1, Pallas kernels: none -> 70.8 us  [fused_layer(): pl.pallas_call(functools.partial(layer_kernel, pieces), out_shape=jax.Sha...]
    all_gather x1 -> x0, waiting for transfers between devices: 37.4 us -> none  [on_device(): lax.all_gather(attended, 'dev', axis=0, tiled=True)]
    scatter x1 -> x0, local copies, waits for them, and re-layouts: 34.4 us -> none  [on_device(): outgoing = jnp.zeros((experts, head_count * capacity, width), jnp.bfloat1...]
    unnamed x3 -> x0, waiting for transfers between devices: 28.8 us -> none
    all_gather x2 -> x0, blocking collectives: 10.2 us -> none  [the longest x1 5.23 us: on_device(): lax.all_gather(expert_ids, 'head', axis=0, tiled=True)]
    all_to_all x1 -> x0, waiting for transfers between devices: 8.23 us -> none  [on_device(): lax.all_to_all(columns, ('dev', 'head'), split_axis=0, concat_axis=1, til...]
    dot_general x4 -> x0, matrix products: 7.74 us -> none  [the longest x1 3.95 us: on_device(): jnp.dot(lax.all_gather(attended, 'dev', axis=0, tiled=True), out_proj, pr...]
  transfers between devices with their start and end apart: 3 -> 0, of which waited for: 3 -> 0; matrix products, arithmetic and copies ran while one was open for 1% -> 0% of each run, Pallas kernels for 0% -> 0%
where the time goes in v1:
time: 79.7 us; the launch traced here: 79.3 us
  Pallas kernels  70.8 us (89%)
  matrix products  4.39 us (6%)
  local copies, waits for them, and re-layouts  2.18 us (3%)
  other arithmetic  1.88 us (2%)
    pallas_call x1, Pallas kernels, fused_layer(): pl.pallas_call(functools.partial(layer_kernel, pieces), out_shape=jax.Sha...  70.8 us
    unnamed x4, local copies, waits for them, and re-layouts  2.18 us
    dot_general x1, matrix products, attend_block(): jnp.einsum('bhgt,bthd->bhgd', weights, value_rows, preferred_element_type...  1.68 us
    dot_general x1, matrix products, attend_block(): jnp.einsum('bhgd,bthd->bhgt', query_f, key_rows.astype(jnp.float32))  1.65 us

profile of v1, /device:TPU:0, one launch (start us, length us, event | category | flops | bytes accessed | tf_op | source)
XLA Modules:
  0.0 79.3 jit_solution(1102318994532532230)
XLA Ops:
  0.0 0.0 copy-start
  0.0 0.8 %iota_compare_fusion = pred[16,128]{1,0:T(8,128)(4,1)S(1)} fusion(s32[16]{0:T(128)} %param.20), kind=kLoop, calls=%fused_computation.17 | loop fusion | flops 2048 | bytes 2112 | tf_op jit(solution)/shard_map/lt | solution.py:24
  0.8 1.1 %fusion.7 = f32[16,2,1,16]{3,2,1,0:T(1,128)S(1)} fusion(bf16[16,2,16,128]{3,2,1,0:T(8,128)(2,1)} %bitcast.19, bf16[16,2,128,1]{2,1,0,3:T(2,128)(2,1)} %bitcast.25), kind=kOutput, calls=%fused_computation.12 | convolution fusion | flops 131072 | bytes 141312 | tf_op jit(solution)/shard_map/bhgd,bhd->bhg/dot_general | solution.py:22
  1.9 0.7 convert_element_type.21
  2.6 0.0 copy-done
  2.6 1.7 %fusion.11 = (f32[16,2,16]{2,1,0:T(2,128)S(1)}, f32[16,2,16,128]{3,2,1,0:T(8,128)S(1)}) fusion(bf16[16,2,16,128]{3,2,1,0:T(8,128)(2,1)} %bitcast.20, bf16[16,128,2,128]{3,2,1,0:T(2,128)(2,1)S(1)} %copy-done, pred[16,128]{1,0:T(8,128)(4,1)S(1)} %iota_compare_fusion), kind=kOutput, calls=%fused_computation.20 | convolution fusion | flops 16973312 | bytes 1445888 | tf_op jit(solution)/shard_map/bhgd,bthd->bhgt/dot_general | solution.py:21
  4.3 0.3 fusion.4
  4.6 1.7 %fusion.1 = bf16[16,2,16,128]{3,2,1,0:T(8,128)(2,1)S(1)} fusion(bf16[16,128,2,128]{3,2,1,0:T(2,128)(2,1)} %param.17, f32[16,2,16,128]{3,2,1,0:T(8,128)S(1)} %get-tuple-element.8, f32[16,2,128]{2,1,0:T(2,128)S(1)} %convert_element_type.21, f32[16,2,16]{2,1,0:T(2,128)S(1)} %get-tuple-element.6, f32[16,2,16]{2,1,0:T(2,128)S(1)} %get-tuple-element.5, ...), kind=kOutput, calls=%fused_computation.3 | convolution fusion | flops 17170432 | bytes 1464320 | tf_op jit(solution)/shard_map/bhgt,bthd->bhgd/dot_general | solution.py:32
  6.3 0.7 copy.29
  7.0 70.8 %shard_map.136 = bf16[8,4096]{1,0:T(8,128)(2,1)} custom-call(bf16[16,4096]{1,0:T(8,128)(2,1)} %bitcast.18, bf16[8,4096]{1,0:T(8,128)(2,1)} %hidden_ref.1, f32[1,4096]{1,0:T(1,128)} %bitcast.24, s32[8,8]{1,0:T(8,128)} %ids_ref.1, s32[8,8]{1,0:T(8,128)} %levels_ref.1, bf16[4096,512]{1,0:T(8,128)(2,1)} %proj_hbm.1, bf16[4096,384]{1,0:T(8,128)(2,1)} %bitcast.15, ...), custom_call_target="tpu_custom_call" | custom-call | flops 2415919104 | bytes 16777216 | tf_op jit(solution)/shard_map/pallas_call | solution.py:422
  77.9 1.5 %copy.31 = bf16[8,4096]{1,0:T(8,128)(2,1)} copy(bf16[8,4096]{1,0:T(8,128)(2,1)} %shard_map.136) | data formatting | bytes 131072
  (2 shorter events, 0.1 us)
Async XLA Ops:
  0.0 2.6 %copy-start = (bf16[16,128,2,128]{3,2,1,0:T(2,128)(2,1)S(1)}, bf16[16,128,2,128]{3,2,1,0:T(2,128)(2,1)}, u32[]{:S(2)}) copy-start(bf16[16,128,2,128]{3,2,1,0:T(2,128)(2,1)} %param.16) | copy-start | bytes 3145732

commit v2 on v1

--- a/solution.py
+++ b/solution.py
@@ -61,7 +61,12 @@
 
 def layer_kernel(
     pieces,
-    att_ref,
+    query_ref,
+    new_key_ref,
+    new_value_ref,
+    length_ref,
+    keys_hbm,
+    values_hbm,
     hidden_ref,
     gain_ref,
     ids_ref,
@@ -71,7 +76,12 @@
     up_hbm,
     down_hbm,
     out_ref,
+    keys_ref,
+    values_ref,
+    att_ref,
     gathered,
+    att_low,
+    att_high,
     proj_ref,
     gate_ref,
     up_ref,
@@ -82,6 +92,7 @@
     token_ref,
     low_ref,
     high_ref,
+    active_ref,
     part_ref,
     core_in,
     first_out,
@@ -101,7 +112,8 @@
     sum_recv,
 ):
     role, dev, head = lax.axis_index("role"), lax.axis_index("dev"), lax.axis_index("head")
-    group_count = gathered.shape[0]
+    group_count = gathered.shape[1]
+    tokens = residual_ref.shape[0]
     width = residual_ref.shape[1]
     half = width // 2
     member = dev * 2 + head
@@ -115,10 +127,17 @@
     loads = [
         pltpu.make_async_copy(source, target, weight_sems.at[number])
         for number, (source, target) in enumerate(
-            ((proj_hbm, proj_ref), (gate_hbm, gate_ref), (up_hbm, up_ref), (down_hbm, down_ref))
-        )
-    ]
-    for load in loads:
+            (
+                (proj_hbm, proj_ref),
+                (gate_hbm, gate_ref),
+                (up_hbm, up_ref),
+                (down_hbm, down_ref),
+                (keys_hbm, keys_ref),
+                (values_hbm, values_ref),
+            )
+        )
+    ]
+    for load in loads[4:] + loads[:4]:
         load.start()
 
     barrier = pltpu.get_barrier_semaphore()
@@ -132,37 +151,119 @@
 
     lax.fori_loop(1, members, greet, 0)
     pl.semaphore_signal(barrier, inc=1, device_id=other_core, device_id_type=MESH)
-    gathered[dev] = att_ref[...]
-    pl.semaphore_wait(barrier, members)
-
-    def att_copy(depth_from, target, number):
-        block = gathered.at[2 * depth_from + low]
+
+    heads, head_dim = query_ref.shape[1:]
+    slots = keys_ref.shape[1]
+    shared = heads // 2
+    scaling = 1.0 / math.sqrt(head_dim)
+    column = lax.broadcasted_iota(jnp.int32, (heads, slots), 1)
+    same_head = column % 2 == lax.broadcasted_iota(jnp.int32, (heads, slots), 0) // shared
+    new_keys = new_key_ref[...].astype(jnp.float32)
+    new_values = new_value_ref[...].astype(jnp.float32)
+
+    def both_heads(rows, request):
+        return jnp.concatenate(
+            [
+                jnp.broadcast_to(rows[2 * request + kv : 2 * request + kv + 1], (shared, head_dim))
+                for kv in range(2)
+            ],
+            axis=0,
+        )
+
+    def attend(request):
+        query = query_ref[request]
+        scores = lax.dot_general(
+            query,
+            keys_ref[request],
+            (((1,), (1,)), ((), ())),
+            preferred_element_type=jnp.float32,
+        )
+        score_new = scaling * jnp.sum(
+            query.astype(jnp.float32) * both_heads(new_keys, request), axis=1, keepdims=True
+        )
+        valid = same_head & (column < 2 * length_ref[request : request + 1, :])
+        masked = jnp.where(valid, scores * scaling, -1e30)
+        highest = jnp.maximum(jnp.max(masked, axis=1, keepdims=True), score_new)
+        terms = jnp.exp(masked - highest)
+        term_new = jnp.exp(score_new - highest)
+        totals = jnp.sum(terms, axis=1, keepdims=True) + term_new
+        weights = (terms / totals).astype(jnp.bfloat16)
+        weight_new = (term_new / totals).astype(jnp.bfloat16).astype(jnp.float32)
+        blended = jnp.dot(weights, values_ref[request], preferred_element_type=jnp.float32)
+        att_ref[request * heads : (request + 1) * heads] = blended + weight_new * both_heads(
+            new_values, request
+        )
+
+    def attend_half(part):
+        for request in range(part * tokens, (part + 1) * tokens):
+            attend(request)
+        for j in range(shared):
+            pair = [
+                att_ref[pl.ds(part * tokens * heads + kv * shared + j, tokens, stride=heads), :]
+                for kv in range(2)
+            ]
+            gathered[part, dev, :, j * head_dim : (j + 1) * head_dim] = jnp.concatenate(
+                pair, axis=0
+            ).astype(jnp.bfloat16)
+
+    def att_copy(part, depth_from, target, number):
+        block = gathered.at[part, 2 * depth_from + low]
         return pltpu.make_async_remote_copy(
             src_ref=block,
             dst_ref=block,
-            send_sem=att_send.at[number],
-            recv_sem=att_recv.at[number],
+            send_sem=att_send.at[7 * part + number],
+            recv_sem=att_recv.at[7 * part + number],
             device_id=target,
             device_id_type=MESH,
         )
 
     beside = (role, 2 * depth + 1 - low, head)
-    along = [att_copy(depth, (role, 2 * depths[k] + low, head), k - 1) for k in (1, 2, 3)]
-    across = [att_copy(depths[k], beside, 3 + k) for k in range(4)]
-    across[0].start()
-    for copy in along:
-        copy.start()
-    for k in (1, 2, 3):
-        along[k - 1].wait_recv()
-        across[k].start()
-    for copy in across:
-        copy.wait_recv()
+    along = [
+        [att_copy(part, depth, (role, 2 * depths[k] + low, head), k - 1) for k in (1, 2, 3)]
+        for part in range(2)
+    ]
+    across = [
+        [att_copy(part, depths[k], beside, 3 + k) for k in range(4)] for part in range(2)
+    ]
+    loads[4].wait()
+    loads[5].wait()
+    for part in range(2):
+        attend_half(part)
+        if part == 0:
+            pl.semaphore_wait(barrier, members)
+        across[part][0].start()
+        for copy in along[part]:
+            copy.start()
+
+    def unfold_att(block):
+        one = gathered[0, block].astype(jnp.float32)
+        two = gathered[1, block].astype(jnp.float32)
+        att_low[block] = jnp.concatenate([one[:tokens], two[:tokens]], axis=0).astype(jnp.bfloat16)
+        att_high[block] = jnp.concatenate([one[tokens:], two[tokens:]], axis=0).astype(
+            jnp.bfloat16
+        )
+
+    for part in range(2):
+        for k in (1, 2, 3):
+            along[part][k - 1].wait_recv()
+            across[part][k].start()
+    for k in range(4):
+        unfold_att(2 * depths[k] + low)
+    for k in range(4):
+        across[0][k].wait_recv()
+    for k in range(4):
+        across[1][k].wait_recv()
+        unfold_att(2 * depths[k] + 1 - low)
 
     loads[0].wait()
-    rows = gathered[...].reshape(group_count * gathered.shape[1], gathered.shape[2])
-    columns = jnp.dot(rows, proj_ref[...], preferred_element_type=jnp.float32)
+    fold = att_low.shape[2]
+    rows = group_count * 2 * tokens
+    columns = jnp.dot(
+        att_low[...].reshape(rows, fold), proj_ref[:fold], preferred_element_type=jnp.float32
+    ) + jnp.dot(
+        att_high[...].reshape(rows, fold), proj_ref[fold:], preferred_element_type=jnp.float32
+    )
     col_width = columns.shape[1]
-    tokens = residual_ref.shape[0]
     columns = columns.reshape(members, tokens, col_width)
     col_out[...] = jnp.concatenate(
         [columns[:, :, : col_width // 2], columns[:, :, col_width // 2 :]], axis=1
@@ -181,6 +282,10 @@
 
     def col_start(step, carry):
         col_copy(step).start()
+        return carry
+
+    def col_sent(step, carry):
+        col_copy(step).wait_send()
         return carry
 
     def col_arrive(step, carry):
@@ -254,18 +359,6 @@
         to_second[k].start()
         to_first[k].start()
     to_core[0].start()
-    for k in range(4):
-        to_second[k].wait_recv()
-        to_first[4 + k].start()
-    to_core[1].start()
-    for k in range(4):
-        to_first[k].wait_recv()
-    to_core[2].start()
-    for k in range(4, 8):
-        to_first[k].wait_recv()
-    to_core[3].start()
-    for copy in to_core:
-        copy.wait_recv()
 
     def unfold(pair, carry):
         one = token_ref[2 * pair, :, :half].astype(jnp.float32)
@@ -274,28 +367,70 @@
         high_ref[pair] = jnp.concatenate([one[tokens:], two[tokens:]], axis=0).astype(jnp.bfloat16)
         return carry
 
+    def unfold_from(role_at, first_at, second_at):
+        start = role_at * 8 + first_at * 4 + second_at * 2
+        lax.fori_loop(start, start + 2, unfold, 0)
+
     pairs = low_ref.shape[0]
-    lax.fori_loop(0, pairs, unfold, 0)
     total_rows = pairs * 2 * tokens
+    set_rows = total_rows // 4
+    set_pairs = pairs // 4
+
+    def expert_set(first_own, first_other):
+        sides = []
+        for ref in (low_ref, high_ref):
+            both = [
+                ref[pl.ds(role * 8 + first_own * 4, set_pairs)],
+                ref[pl.ds((1 - role) * 8 + first_other * 4, set_pairs)],
+            ]
+            sides.append(jnp.concatenate(both, axis=0).reshape(2 * set_rows, half))
+
+        def through(weight_ref):
+            return jnp.dot(
+                sides[0], weight_ref[:half], preferred_element_type=jnp.float32
+            ) + jnp.dot(sides[1], weight_ref[half:], preferred_element_type=jnp.float32)
+
+        gate_part = through(gate_ref)
+        up_part = through(up_ref)
+        active = (gate_part / (1.0 + jnp.exp(-gate_part)) * up_part).astype(jnp.bfloat16)
+        active_ref[role * 2 + first_own] = active[:set_rows]
+        active_ref[(1 - role) * 2 + first_other] = active[set_rows:]
+
+    unfold_from(role, first, second)
+    for k in range(4):
+        to_second[k].wait_recv()
+        to_first[4 + k].start()
+    to_core[1].start()
+    unfold_from(role, first, 1 - second)
+    lax.fori_loop(1, members, col_sent, 0)
+    for part in range(2):
+        for copy in along[part] + across[part]:
+            copy.wait_send()
+    for load in loads[1:4]:
+        load.wait()
+    for k in range(4):
+        to_first[k].wait_recv()
+    to_core[2].start()
+    unfold_from(role, 1 - first, second)
+    to_core[0].wait_recv()
+    unfold_from(1 - role, second, first)
+    to_core[1].wait_recv()
+    unfold_from(1 - role, second, 1 - first)
+    expert_set(first, second)
+    for k in range(4, 8):
+        to_first[k].wait_recv()
+    to_core[3].start()
+    unfold_from(role, 1 - first, 1 - second)
+    to_core[2].wait_recv()
+    unfold_from(1 - role, 1 - second, first)
+    to_core[3].wait_recv()
+    unfold_from(1 - role, 1 - second, 1 - first)
+    expert_set(1 - first, 1 - second)
     table = token_ref[:, :, half:].astype(jnp.float32)[:, :tokens].reshape(total_rows, 128)
     mine = lax.broadcasted_iota(jnp.int32, (total_rows, 128), 1) == role * group_count + dev
     share = jnp.sum(jnp.where(mine, table, 0.0), axis=1, keepdims=True) / jnp.sum(
         table, axis=1, keepdims=True
     )
-    left = low_ref[...].reshape(total_rows, half)
-    right = high_ref[...].reshape(total_rows, half)
-
-    def through(weight_ref):
-        return jnp.dot(left, weight_ref[:half], preferred_element_type=jnp.float32) + jnp.dot(
-            right, weight_ref[half:], preferred_element_type=jnp.float32
-        )
-
-    loads[1].wait()
-    gate_part = through(gate_ref)
-    loads[2].wait()
-    up_part = through(up_ref)
-    active = (gate_part / (1.0 + jnp.exp(-gate_part)) * up_part).astype(jnp.bfloat16)
-    loads[3].wait()
 
     span_width = half // pieces
 
@@ -332,12 +467,14 @@
         for p in range(pieces)
     ]
 
+    active_rows = active_ref[...].reshape(total_rows, active_ref.shape[2])
+
     def produce(p):
         sides = []
         for side in range(2):
             edge = side * half + p * span_width
             product = jnp.dot(
-                active, down_ref[:, edge : edge + span_width], preferred_element_type=jnp.float32
+                active_rows, down_ref[:, edge : edge + span_width], preferred_element_type=jnp.float32
             )
             sides.append((product * share).reshape(2 * pairs, tokens, span_width))
         part_ref[p] = jnp.concatenate(sides, axis=1).astype(jnp.bfloat16)
@@ -383,34 +520,52 @@
             span = slice(edge, edge + span_width)
             out_ref[:, span] = (
                 residual_ref[:, span] + total[side * tokens : (side + 1) * tokens]
-            ).astype(jnp.bfloat16)
+            )
+
+    sent = to_depth + to_second + to_first + to_core
+
+    def settle(p):
+        share_of = -(-len(sent) // pieces)
+        for copy in sent[p * share_of : (p + 1) * share_of]:
+            copy.wait_send()
+        for copy in (core_sums[p], first_sums[p], second_sums[p]):
+            copy.wait_send()
 
     steps = (produce, pass_first, pass_second, pass_depth, finish)
     for turn in range(pieces + len(steps) - 1):
         for lag, step in enumerate(steps):
             if 0 <= turn - lag < pieces:
                 step(turn - lag)
-
-    def col_sent(step, carry):
-        col_copy(step).wait_send()
-        return carry
-
-    lax.fori_loop(1, members, col_sent, 0)
-    sent = along + across + to_depth + to_second + to_first + to_core
-    sent = sent + core_sums + first_sums + second_sums
+                if step is pass_depth:
+                    settle(turn - lag)
+
     for group in depth_sums:
-        sent = sent + group
-    for copy in sent:
-        copy.wait_send()
+        for copy in group:
+            copy.wait_send()
 
 
 def fused_layer(
-    attended, hidden, norm_gain, expert_ids, gate_levels, out_proj, gate_w, up_w, down_w
+    queries,
+    new_keys,
+    new_values,
+    lengths,
+    cache_keys,
+    cache_values,
+    hidden,
+    norm_gain,
+    expert_ids,
+    gate_levels,
+    out_proj,
+    gate_w,
+    up_w,
+    down_w,
 ):
     pieces = 4
     tokens, width = hidden.shape
     half = width // 2
-    rows, inner = attended.shape
+    rows, heads, head_dim = queries.shape
+    inner = heads * head_dim
+    cached = cache_keys.shape[1] * cache_keys.shape[2]
     col_width = out_proj.shape[1]
     dev_count = lax.axis_size("dev")
     hidden_units = gate_w.shape[1]
@@ -419,13 +574,18 @@
     vmem = pl.BlockSpec(memory_space=pltpu.VMEM)
     anywhere = pl.BlockSpec(memory_space=pl.ANY)
     sems = pltpu.SemaphoreType.DMA
-    return pl.pallas_call(
+    out = pl.pallas_call(
         functools.partial(layer_kernel, pieces),
-        out_shape=jax.ShapeDtypeStruct((tokens, width), bf16),
-        in_specs=[vmem] * 5 + [anywhere] * 4,
+        out_shape=jax.ShapeDtypeStruct((tokens, width), jnp.float32),
+        in_specs=[vmem] * 4 + [anywhere] * 2 + [vmem] * 4 + [anywhere] * 4,
         out_specs=vmem,
         scratch_shapes=[
-            pltpu.VMEM((dev_count, rows, inner), bf16),
+            pltpu.VMEM((rows, cached, head_dim), bf16),
+            pltpu.VMEM((rows, cached, head_dim), bf16),
+            pltpu.VMEM((rows * heads, head_dim), jnp.float32),
+            pltpu.VMEM((2, dev_count, rows, inner // 2), bf16),
+            pltpu.VMEM((dev_count, rows, inner // 2), bf16),
+            pltpu.VMEM((dev_count, rows, inner // 2), bf16),
             pltpu.VMEM(out_proj.shape, bf16),
             pltpu.VMEM((width, hidden_units), bf16),
             pltpu.VMEM((width, hidden_units), bf16),
@@ -436,6 +596,7 @@
             pltpu.VMEM((4 * dev_count, 2 * tokens, half + 128), bf16),
             pltpu.VMEM((2 * dev_count, 2 * tokens, half), bf16),
             pltpu.VMEM((2 * dev_count, 2 * tokens, half), bf16),
+            pltpu.VMEM((4, 8 * tokens, hidden_units), bf16),
             pltpu.VMEM((pieces, 32, 2 * tokens, span), bf16),
             pltpu.VMEM((pieces, 16, 2 * tokens, span), bf16),
             pltpu.VMEM((pieces, 8, 2 * tokens, span), bf16),
@@ -444,9 +605,9 @@
             pltpu.VMEM((pieces, 4, 2 * tokens, span), bf16),
             pltpu.VMEM((pieces, 3, 2 * tokens, span), bf16),
             pltpu.VMEM((pieces, 3, 2 * tokens, span), bf16),
-            sems((4,)),
-            sems((7,)),
-            sems((7,)),
+            sems((6,)),
+            sems((14,)),
+            sems((14,)),
             sems((2 * dev_count - 1,)),
             sems((2 * dev_count - 1,)),
             sems((19,)),
@@ -461,7 +622,12 @@
             flops=3 * 2 * 256 * width * hidden_units, bytes_accessed=16 << 20, transcendentals=0
         ),
     )(
-        attended,
+        queries,
+        new_keys.reshape(2 * rows, head_dim),
+        new_values.reshape(2 * rows, head_dim),
+        lengths.reshape(rows, 1),
+        cache_keys.reshape(rows, cached, head_dim),
+        cache_values.reshape(rows, cached, head_dim),
         hidden,
         norm_gain.reshape(1, width),
         expert_ids,
@@ -471,6 +637,7 @@
         up_w,
         down_w,
     )
+    return out.astype(bf16)
 
 
 def on_device(
@@ -489,11 +656,15 @@
     expert_ids,
     gate_levels,
 ):
-    attended = attend_block(queries, cache_keys, cache_values, new_keys, new_values, lengths)
     sizes = tuple(lax.axis_size(name) for name in ("role", "dev", "head"))
     if sizes == (2, 8, 2) and hidden.shape[0] == 8 and queries.shape[0] == 16:
         return fused_layer(
-            attended,
+            queries,
+            new_keys,
+            new_values,
+            lengths,
+            cache_keys,
+            cache_values,
             hidden,
             norm_gain,
             expert_ids,
@@ -503,6 +674,7 @@
             expert_up[0],
             expert_down[0],
         )
+    attended = attend_block(queries, cache_keys, cache_values, new_keys, new_values, lengths)
     columns = jnp.dot(
         lax.all_gather(attended, "dev", axis=0, tiled=True),
         out_proj,

time: 79.7 us -> 72.8 us (0.913)
  matrix products: 4.39 us -> 0 us
  Pallas kernels: 70.8 us -> 69.7 us
  local copies, waits for them, and re-layouts: 2.18 us -> 1.33 us
    dot_general x3 -> x0, matrix products: 4.39 us -> none  [the longest x1 1.68 us: attend_block(): jnp.einsum('bhgt,bthd->bhgd', weights, value_rows, preferred_element_type...]
    unnamed x4 -> x0, local copies, waits for them, and re-layouts: 2.18 us -> none
    reshape x0 -> x1, local copies, waits for them, and re-layouts: none -> 1.33 us  [fused_layer(): lengths.reshape(rows, 1)]
    pallas_call x1, Pallas kernels: 70.8 us -> 69.7 us  [fused_layer(): pl.pallas_call(functools.partial(layer_kernel, pieces), out_shape=jax.Sha...]
    convert_element_type x1, other arithmetic: 0.73 us -> 1.54 us  [fused_layer(): return out.astype(bf16)]
    lt x1 -> x0, other arithmetic: 0.82 us -> none  [attend_block(): usable = (positions[None, :] < valid_len[:, None])[:, None, None, :]]
where the time goes in v2:
time: 72.8 us; the launch traced here: 72.6 us
  Pallas kernels  69.7 us (96%)
  other arithmetic  1.54 us (2%)
  local copies, waits for them, and re-layouts  1.33 us (2%)
    pallas_call x1, Pallas kernels, fused_layer(): pl.pallas_call(functools.partial(layer_kernel, pieces), out_shape=jax.Sha...  69.7 us
    convert_element_type x1, other arithmetic, fused_layer(): return out.astype(bf16)  1.54 us

profile of v2, /device:TPU:0, one launch (start us, length us, event | category | flops | bytes accessed | tf_op | source)
XLA Modules:
  0.0 72.6 jit_solution(17075866020539540892)
XLA Ops:
  0.0 1.3 %copy.15.length_ref = s32[16,1]{1,0:T(8,128)} copy(s32[16,1]{0,1:T(1,128)} %bitcast.17) | data formatting | bytes 128 | tf_op jit(solution)/shard_map/reshape | solution.py:628
  1.3 69.7 %shard_map.136 = f32[8,4096]{1,0:T(8,128)} custom-call(bf16[16,32,128]{2,1,0:T(8,128)(2,1)} %query_ref.1, bf16[32,128]{1,0:T(8,128)(2,1)} %bitcast.15, bf16[32,128]{1,0:T(8,128)(2,1)} %bitcast.16, s32[16,1]{1,0:T(8,128)} %copy.15.length_ref, bf16[16,256,128]{2,1,0:T(8,128)(2,1)} %bitcast.12, bf16[16,256,128]{2,1,0:T(8,128)(2,1)} %bitcast.13, ...), custom_call_target="tpu_custom_call" | custom-call | flops 2415919104 | bytes 16777216 | tf_op jit(solution)/shard_map/pallas_call | solution.py:577
  71.1 1.5 %convert_element_type.3 = bf16[8,4096]{1,0:T(8,128)(2,1)} convert(f32[8,4096]{1,0:T(8,128)} %shard_map.136) | non-fusion elementwise | flops 32768 | bytes 196608 | tf_op jit(solution)/shard_map/convert_element_type | solution.py:640

commit v3 on v2

--- a/solution.py
+++ b/solution.py
@@ -181,7 +181,7 @@
         score_new = scaling * jnp.sum(
             query.astype(jnp.float32) * both_heads(new_keys, request), axis=1, keepdims=True
         )
-        valid = same_head & (column < 2 * length_ref[request : request + 1, :])
+        valid = same_head & (column < 2 * length_ref[request])
         masked = jnp.where(valid, scores * scaling, -1e30)
         highest = jnp.maximum(jnp.max(masked, axis=1, keepdims=True), score_new)
         terms = jnp.exp(masked - highest)
@@ -294,6 +294,15 @@
 
     lax.fori_loop(1, members, col_start, 0)
     col_in[member] = col_out[member]
+    lanes = lax.broadcasted_iota(jnp.int32, (tokens, 128), 1)
+    named = jnp.zeros((tokens, 128), jnp.float32)
+    for k in range(ids_ref.shape[1]):
+        level = levels_ref[:, k : k + 1].astype(jnp.float32)
+        named = named + jnp.where(lanes == ids_ref[:, k : k + 1], level, 0.0)
+    slot = role * 16 + first * 8 + second * 4 + depth
+    token_ref[slot, :, half:] = jnp.concatenate(
+        [named, jnp.zeros((tokens, 128), jnp.float32)], axis=0
+    ).astype(jnp.bfloat16)
     lax.fori_loop(1, members, col_arrive, 0)
 
     for block in range(group_count):
@@ -307,17 +316,8 @@
     residual = residual_ref[...]
     square = jnp.sum(residual * residual, axis=-1, keepdims=True) / width
     normed = residual * lax.rsqrt(square + 1e-06) * gain_ref[...]
-    lanes = lax.broadcasted_iota(jnp.int32, (tokens, 128), 1)
-    named = jnp.zeros((tokens, 128), jnp.float32)
-    for k in range(ids_ref.shape[1]):
-        level = levels_ref[:, k : k + 1].astype(jnp.float32)
-        named = named + jnp.where(lanes == ids_ref[:, k : k + 1], level, 0.0)
-    slot = role * 16 + first * 8 + second * 4 + depth
     token_ref[slot, :, :half] = jnp.concatenate(
         [normed[:, :half], normed[:, half:]], axis=0
-    ).astype(jnp.bfloat16)
-    token_ref[slot, :, half:] = jnp.concatenate(
-        [named, jnp.zeros((tokens, 128), jnp.float32)], axis=0
     ).astype(jnp.bfloat16)
 
     def token_copy(start, count, target, number):
@@ -354,11 +354,16 @@
     to_first[0].start()
     for copy in to_depth:
         copy.start()
-    for k in (1, 2, 3):
-        to_depth[k - 1].wait_recv()
-        to_second[k].start()
-        to_first[k].start()
-    to_core[0].start()
+    for k in range(4):
+        if k > 0:
+            to_depth[k - 1].wait_recv()
+            to_second[k].start()
+            to_first[k].start()
+            if k == 3:
+                to_core[0].start()
+        if k < 3:
+            to_second[k].wait_recv()
+            to_first[4 + k].start()
 
     def unfold(pair, carry):
         one = token_ref[2 * pair, :, :half].astype(jnp.float32)
@@ -397,9 +402,8 @@
         active_ref[(1 - role) * 2 + first_other] = active[set_rows:]
 
     unfold_from(role, first, second)
-    for k in range(4):
-        to_second[k].wait_recv()
-        to_first[4 + k].start()
+    to_second[3].wait_recv()
+    to_first[7].start()
     to_core[1].start()
     unfold_from(role, first, 1 - second)
     lax.fori_loop(1, members, col_sent, 0)
@@ -411,15 +415,15 @@
     for k in range(4):
         to_first[k].wait_recv()
     to_core[2].start()
-    unfold_from(role, 1 - first, second)
     to_core[0].wait_recv()
     unfold_from(1 - role, second, first)
     to_core[1].wait_recv()
     unfold_from(1 - role, second, 1 - first)
-    expert_set(first, second)
+    unfold_from(role, 1 - first, second)
     for k in range(4, 8):
         to_first[k].wait_recv()
     to_core[3].start()
+    expert_set(first, second)
     unfold_from(role, 1 - first, 1 - second)
     to_core[2].wait_recv()
     unfold_from(1 - role, 1 - second, first)
@@ -531,14 +535,19 @@
         for copy in (core_sums[p], first_sums[p], second_sums[p]):
             copy.wait_send()
 
-    steps = (produce, pass_first, pass_second, pass_depth, finish)
-    for turn in range(pieces + len(steps) - 1):
-        for lag, step in enumerate(steps):
-            if 0 <= turn - lag < pieces:
-                step(turn - lag)
-                if step is pass_depth:
-                    settle(turn - lag)
-
+    for p in range(pieces):
+        produce(p)
+        if p > 1:
+            pass_first(p - 2)
+    for p in range(max(pieces - 2, 0), pieces):
+        pass_first(p)
+    for p in range(pieces):
+        pass_second(p)
+    for p in range(pieces):
+        pass_depth(p)
+        settle(p)
+    for p in range(pieces):
+        finish(p)
     for group in depth_sums:
         for copy in group:
             copy.wait_send()
@@ -572,12 +581,13 @@
     span = half // pieces
     bf16 = jnp.bfloat16
     vmem = pl.BlockSpec(memory_space=pltpu.VMEM)
+    scalars = pl.BlockSpec(memory_space=pltpu.SMEM)
     anywhere = pl.BlockSpec(memory_space=pl.ANY)
     sems = pltpu.SemaphoreType.DMA
     out = pl.pallas_call(
         functools.partial(layer_kernel, pieces),
         out_shape=jax.ShapeDtypeStruct((tokens, width), jnp.float32),
-        in_specs=[vmem] * 4 + [anywhere] * 2 + [vmem] * 4 + [anywhere] * 4,
+        in_specs=[vmem] * 3 + [scalars] + [anywhere] * 2 + [vmem] * 4 + [anywhere] * 4,
         out_specs=vmem,
         scratch_shapes=[
             pltpu.VMEM((rows, cached, head_dim), bf16),
@@ -625,7 +635,7 @@
         queries,
         new_keys.reshape(2 * rows, head_dim),
         new_values.reshape(2 * rows, head_dim),
-        lengths.reshape(rows, 1),
+        lengths,
         cache_keys.reshape(rows, cached, head_dim),
         cache_values.reshape(rows, cached, head_dim),
         hidden,

time: 72.8 us -> 75.3 us (1.034)
  Pallas kernels: 69.7 us -> 73.6 us
  local copies, waits for them, and re-layouts: 1.33 us -> 0 us
    pallas_call x1, Pallas kernels: 69.7 us -> 73.6 us  [fused_layer(): pl.pallas_call(functools.partial(layer_kernel, pieces), out_shape=jax.Sha...]
    reshape x1 -> x0, local copies, waits for them, and re-layouts: 1.33 us -> none  [fused_layer(): lengths.reshape(rows, 1)]
where the time goes in v3:
time: 75.3 us; the launch traced here: 75.1 us
  Pallas kernels  73.6 us (98%)
  other arithmetic  1.54 us (2%)
    pallas_call x1, Pallas kernels, fused_layer(): pl.pallas_call(functools.partial(layer_kernel, pieces), out_shape=jax.Sha...  73.6 us
    convert_element_type x1, other arithmetic, fused_layer(): return out.astype(bf16)  1.54 us

profile of v3, /device:TPU:0, one launch (start us, length us, event | category | flops | bytes accessed | tf_op | source)
XLA Modules:
  0.0 75.1 jit_solution(883503024492407245)
XLA Ops:
  0.0 73.6 %shard_map.136 = f32[8,4096]{1,0:T(8,128)} custom-call(bf16[16,32,128]{2,1,0:T(8,128)(2,1)} %query_ref.1, bf16[32,128]{1,0:T(8,128)(2,1)} %bitcast.14, bf16[32,128]{1,0:T(8,128)(2,1)} %bitcast.15, s32[16]{0:T(128)} %length_ref.1, bf16[16,256,128]{2,1,0:T(8,128)(2,1)} %bitcast.11, bf16[16,256,128]{2,1,0:T(8,128)(2,1)} %bitcast.12, ...), custom_call_target="tpu_custom_call" | custom-call | flops 2415919104 | bytes 16777216 | tf_op jit(solution)/shard_map/pallas_call | solution.py:587
  73.6 1.5 %convert_element_type.3 = bf16[8,4096]{1,0:T(8,128)(2,1)} convert(f32[8,4096]{1,0:T(8,128)} %shard_map.136) | non-fusion elementwise | flops 32768 | bytes 196608 | tf_op jit(solution)/shard_map/convert_element_type | solution.py:650

commit v4 on v2

--- a/solution.py
+++ b/solution.py
@@ -181,7 +181,7 @@
         score_new = scaling * jnp.sum(
             query.astype(jnp.float32) * both_heads(new_keys, request), axis=1, keepdims=True
         )
-        valid = same_head & (column < 2 * length_ref[request : request + 1, :])
+        valid = same_head & (column < 2 * length_ref[:, request : request + 1])
         masked = jnp.where(valid, scores * scaling, -1e30)
         highest = jnp.maximum(jnp.max(masked, axis=1, keepdims=True), score_new)
         terms = jnp.exp(masked - highest)
@@ -294,6 +294,15 @@
 
     lax.fori_loop(1, members, col_start, 0)
     col_in[member] = col_out[member]
+    lanes = lax.broadcasted_iota(jnp.int32, (tokens, 128), 1)
+    named = jnp.zeros((tokens, 128), jnp.float32)
+    for k in range(ids_ref.shape[1]):
+        level = levels_ref[:, k : k + 1].astype(jnp.float32)
+        named = named + jnp.where(lanes == ids_ref[:, k : k + 1], level, 0.0)
+    slot = role * 16 + first * 8 + second * 4 + depth
+    token_ref[slot, :, half:] = jnp.concatenate(
+        [named, jnp.zeros((tokens, 128), jnp.float32)], axis=0
+    ).astype(jnp.bfloat16)
     lax.fori_loop(1, members, col_arrive, 0)
 
     for block in range(group_count):
@@ -307,17 +316,8 @@
     residual = residual_ref[...]
     square = jnp.sum(residual * residual, axis=-1, keepdims=True) / width
     normed = residual * lax.rsqrt(square + 1e-06) * gain_ref[...]
-    lanes = lax.broadcasted_iota(jnp.int32, (tokens, 128), 1)
-    named = jnp.zeros((tokens, 128), jnp.float32)
-    for k in range(ids_ref.shape[1]):
-        level = levels_ref[:, k : k + 1].astype(jnp.float32)
-        named = named + jnp.where(lanes == ids_ref[:, k : k + 1], level, 0.0)
-    slot = role * 16 + first * 8 + second * 4 + depth
     token_ref[slot, :, :half] = jnp.concatenate(
         [normed[:, :half], normed[:, half:]], axis=0
-    ).astype(jnp.bfloat16)
-    token_ref[slot, :, half:] = jnp.concatenate(
-        [named, jnp.zeros((tokens, 128), jnp.float32)], axis=0
     ).astype(jnp.bfloat16)
 
     def token_copy(start, count, target, number):
@@ -531,9 +531,9 @@
         for copy in (core_sums[p], first_sums[p], second_sums[p]):
             copy.wait_send()
 
-    steps = (produce, pass_first, pass_second, pass_depth, finish)
-    for turn in range(pieces + len(steps) - 1):
-        for lag, step in enumerate(steps):
+    steps = ((produce, 0), (pass_first, 1), (pass_second, 2), (pass_depth, 3), (finish, 5))
+    for turn in range(pieces + 5):
+        for step, lag in steps:
             if 0 <= turn - lag < pieces:
                 step(turn - lag)
                 if step is pass_depth:
@@ -625,7 +625,7 @@
         queries,
         new_keys.reshape(2 * rows, head_dim),
         new_values.reshape(2 * rows, head_dim),
-        lengths.reshape(rows, 1),
+        lengths.reshape(1, rows),
         cache_keys.reshape(rows, cached, head_dim),
         cache_values.reshape(rows, cached, head_dim),
         hidden,

time: 72.8 us -> 71.5 us (0.982)
  local copies, waits for them, and re-layouts: 1.33 us -> 0 us
    reshape x1 -> x0, local copies, waits for them, and re-layouts: 1.33 us -> none  [fused_layer(): lengths.reshape(rows, 1)]
where the time goes in v4:
time: 71.5 us; the launch traced here: 71.3 us
  Pallas kernels  69.8 us (98%)
  other arithmetic  1.54 us (2%)
    pallas_call x1, Pallas kernels, fused_layer(): pl.pallas_call(functools.partial(layer_kernel, pieces), out_shape=jax.Sha...  69.8 us
    convert_element_type x1, other arithmetic, fused_layer(): return out.astype(bf16)  1.54 us

profile of v4, /device:TPU:0, one launch (start us, length us, event | category | flops | bytes accessed | tf_op | source)
XLA Modules:
  0.0 71.3 jit_solution(940078997646041404)
XLA Ops:
  0.0 69.8 %shard_map.136 = f32[8,4096]{1,0:T(8,128)} custom-call(bf16[16,32,128]{2,1,0:T(8,128)(2,1)} %query_ref.1, bf16[32,128]{1,0:T(8,128)(2,1)} %bitcast.15, bf16[32,128]{1,0:T(8,128)(2,1)} %bitcast.16, s32[1,16]{1,0:T(1,128)} %bitcast.17, bf16[16,256,128]{2,1,0:T(8,128)(2,1)} %bitcast.12, bf16[16,256,128]{2,1,0:T(8,128)(2,1)} %bitcast.13, ...), custom_call_target="tpu_custom_call" | custom-call | flops 2415919104 | bytes 16777216 | tf_op jit(solution)/shard_map/pallas_call | solution.py:577
  69.8 1.5 %convert_element_type.3 = bf16[8,4096]{1,0:T(8,128)(2,1)} convert(f32[8,4096]{1,0:T(8,128)} %shard_map.136) | non-fusion elementwise | flops 32768 | bytes 196608 | tf_op jit(solution)/shard_map/convert_element_type | solution.py:640
